TPU v7x, 32 devices: a whole 2x2x4 slice. The times are simulated.
32 devices in a mesh: patch: 2 (over x), col: 16 (over z, y, core).
Axes of the slice: x: 2, y: 2, z: 4, core: 2. Of those that a mesh axis runs over, the one named last changes fastest.
Arguments:
- sources_field: bfloat16 [8, 2048, 256], P('patch', 'col'), parts along dimension 0, may hold values from -6 to 6
- residual_field: bfloat16 [8, 2048, 256], P('patch', 'col'), parts along dimension 0, may hold values from -6 to 6
- v_factors: bfloat16 [8, 2, 2048, 384], P('patch', None, 'col'), parts along dimension 0, may hold values from -0.25 to 0.25
- u_factors: bfloat16 [8, 2, 2048, 384], P('patch', None, 'col'), parts along dimension 0, may hold values from -0.375 to 0.375
- tile_class: int32 [8, 8, 8], P('patch'), parts along dimension 0, may hold values from 0 to 3, as said below
Outputs:
- forward_field: bfloat16 [8, 2048, 256], P('patch', 'col'), parts along dimension 0
- adjoint_field: bfloat16 [8, 2048, 256], P('patch', 'col'), parts along dimension 0
There are 2 independent parts, one for each index of `patch`. A program takes and returns all parts, laid end to end along the dimension named above; each array names one. Nothing has to cross between parts.
Inputs may be any that keep to these rules, and one draw needn't show every extreme that they name: `tile_class`: in every frequency, every tile row and every tile column holds exactly 2 tiles of class 0, 3 of class 1, 2 of class 2 and 1 of class 3.
All inputs are finite; a program needn't handle non-finite values.
Results may differ from a plain program's by a relative error of at most 0.0058.
Values may be sent and summed in bfloat16 or wider, within the bound.
A program may use at most 128 MiB of HBM per device.

v0:
```python
import jax
import jax.numpy as jnp
from jax import lax
from jax.sharding import PartitionSpec as P

RANK0 = 8
RANK1 = 16
RANK2 = 32
RANK3 = 48


def swapped(value, axis, stride):
    return lax.ppermute(value, axis, [(i, i ^ 1 << stride) for i in range(lax.axis_size(axis))])


def class_widths(classes):
    return (
        (classes == 0).astype(jnp.int32) * RANK0
        + (classes == 1).astype(jnp.int32) * RANK1
        + (classes == 2).astype(jnp.int32) * RANK2
        + (classes == 3).astype(jnp.int32) * RANK3
    )


def partials(source_factor, field_block, tile_widths):
    freq_count, _, half_rows, col_count = source_factor.shape
    tile_count = tile_widths.shape[1]
    rank_width = col_count // tile_count
    point_count = field_block.shape[2] // 2
    stacked = source_factor.reshape(freq_count, 2 * half_rows, col_count)
    real_part = field_block[:, :, :point_count]
    imag_part = field_block[:, :, point_count:]
    lower_rows = jnp.concatenate([imag_part, -real_part], axis=2)
    operand = jnp.concatenate([field_block, lower_rows], axis=1)
    coeffs = jnp.einsum("fnq,fnc->fqc", stacked, operand, preferred_element_type=jnp.float32)
    coeffs = coeffs.reshape(freq_count, tile_count, rank_width, 2, point_count)
    alive_mask = lax.broadcasted_iota(jnp.int32, (1, 1, rank_width), 2) < tile_widths[:, :, None]
    return jnp.where(alive_mask[:, :, :, None, None], coeffs, 0.0).astype(jnp.bfloat16)


def apply_split(target_factor, summed):
    freq_count, _, half_rows, col_count = target_factor.shape
    tile_count = summed.shape[1]
    rank_width = col_count // tile_count
    stacked = target_factor.reshape(freq_count, 2 * half_rows, tile_count, rank_width)
    mixed = jnp.einsum("fnbk,fbgkcp->fngcp", stacked, summed, preferred_element_type=jnp.float32)
    mixed = mixed.reshape(freq_count, 2, half_rows, 2, 2, summed.shape[-1])
    out_real = mixed[:, 0, :, :, 0] - mixed[:, 1, :, :, 1]
    out_imag = mixed[:, 0, :, :, 1] + mixed[:, 1, :, :, 0]
    return jnp.stack([out_real, out_imag], axis=2).astype(jnp.bfloat16)


def carry_over(source_factor, field_block, target_factor, tile_widths, my_side):
    partial_value = partials(source_factor, field_block, tile_widths)
    freq_count, tile_count, rank_width, _, point_count = partial_value.shape
    half_rows = target_factor.shape[2]
    halves = partial_value.reshape(freq_count, tile_count, rank_width, 2, 2, point_count // 2)
    kept_half = lax.dynamic_index_in_dim(halves, my_side, axis=4, keepdims=False)
    given_half = lax.dynamic_index_in_dim(halves, 1 - my_side, axis=4, keepdims=False)
    taken_half = swapped(given_half, "col", 0)
    summed = (kept_half.astype(jnp.float32) + taken_half.astype(jnp.float32)).astype(jnp.bfloat16)
    outgoing = jnp.repeat(summed, 2, axis=1)
    incoming = lax.all_to_all(outgoing, "col", split_axis=1, concat_axis=1, tiled=True)
    grouped = incoming.reshape(incoming.shape[0], tile_count, 2, rank_width, 2, incoming.shape[-1])
    result = apply_split(target_factor, grouped)
    return result.reshape(freq_count, half_rows, 2 * point_count)


def body(sources_field, residual_field, v_factors, u_factors, tile_class):
    my_index = lax.axis_index("col")
    my_block = my_index // 2
    my_side = my_index % 2
    widths = class_widths(tile_class)
    forward_widths = lax.dynamic_index_in_dim(widths, my_block, axis=2, keepdims=False)
    adjoint_widths = lax.dynamic_index_in_dim(widths, my_block, axis=1, keepdims=False)
    forward_field = carry_over(v_factors, sources_field, u_factors, forward_widths, my_side)
    adjoint_field = carry_over(u_factors, residual_field, v_factors, adjoint_widths, my_side)
    return (forward_field, adjoint_field)


def solution(mesh):
    placed = (
        P("patch", "col", None),
        P("patch", "col", None),
        P("patch", None, "col", None),
        P("patch", None, "col", None),
        P("patch", None, None),
    )
    return jax.shard_map(
        body,
        mesh=mesh,
        in_specs=placed,
        out_specs=(P("patch", "col", None), P("patch", "col", None)),
        check_vma=False,
    )
```

profile of v0, /device:TPU:0, one launch (start us, length us, event | category | flops | bytes accessed | tf_op | source)
XLA Modules:
  0.0 85.1 jit_solution(15739334082771763773)
XLA Ops:
  0.6 0.7 select_add_fusion
  1.4 0.2 dynamic-slice_reduce_fusion
  1.7 1.1 %copy.77 = bf16[4,128,256]{1,2,0:T(8,128)(2,1)S(1)} copy(bf16[4,128,256]{2,1,0:T(8,128)(2,1)} %param.5) | data formatting | bytes 524288 | tf_op args[0]
  2.9 1.6 %convolution_bitcast_fusion.1 = bf16[4,384,256]{1,2,0:T(8,128)(2,1)S(1)} fusion(bf16[4,256,384]{2,1,0:T(8,128)(2,1)} %bitcast.89, bf16[4,128,128]{1,2,0:T(8,128)(2,1)S(1)} %get-tuple-element.23, bf16[4,128,128]{1,2,0:T(8,128)(2,1)S(1)} %get-tuple-element.22, bf16[4,128,256]{1,2,0:T(8,128)(2,1)S(1)} %copy.77), kind=kOutput, calls=%fused_computation.11 | convolution fusion | flops 202899456 | bytes 2097152 | tf_op jit(solution)/shard_map/fnq,fnc->fqc/dot_general | solution.py:35
  4.4 0.3 copy.78
  4.7 0.7 reshape.139
  5.5 0.2 copy-done.5
  5.7 0.2 copy.91
  5.9 1.3 %convolution_bitcast_fusion = bf16[4,384,256]{1,2,0:T(8,128)(2,1)} fusion(bf16[4,256,384]{2,1,0:T(8,128)(2,1)S(1)} %bitcast.90, bf16[4,128,128]{1,2,0:T(8,128)(2,1)S(1)} %get-tuple-element.21, bf16[4,128,128]{1,2,0:T(8,128)(2,1)S(1)} %get-tuple-element.20, bf16[4,128,256]{1,2,0:T(8,128)(2,1)S(1)} %copy.91), kind=kOutput, calls=%fused_computation.10 | convolution fusion | flops 202899456 | bytes 2097152 | tf_op jit(solution)/shard_map/fnq,fnc->fqc/dot_general | solution.py:35
  7.3 1.4 %copy.92 = bf16[4,384,256]{2,1,0:T(8,128)(2,1)S(1)} copy(bf16[4,384,256]{1,2,0:T(8,128)(2,1)} %convolution_bitcast_fusion) | data formatting | bytes 1572864 | tf_op jit(solution)/shard_map/fnq,fnc->fqc/dot_general | solution.py:35
  8.7 1.6 %reshape.145 = bf16[4,8,48,2,2,64]{5,4,3,2,1,0:T(2,128)(2,1)} reshape(bf16[4,384,256]{2,1,0:T(8,128)(2,1)S(1)} %copy.92) | data formatting | bytes 1572864 | tf_op jit(solution)/shard_map/reshape | solution.py:36
  10.3 2.3 %select_convert_fusion.1 = bf16[4,8,48,2,2,64]{5,4,3,2,1,0:T(2,128)(2,1)S(1)} fusion(bf16[4,8,48,2,2,64]{5,4,3,2,1,0:T(2,128)(2,1)S(1)} %reshape.139, pred[4,8,48]{2,1,0:T(8,128)(4,1)S(1)} %iota_compare_fusion.1), kind=kLoop, calls=%fused_computation.1 | loop fusion | flops 393216 | bytes 1574400 | tf_op jit(solution)/shard_map/convert_element_type | solution.py:38
  12.6 2.3 %select_convert_fusion = bf16[4,8,48,2,2,64]{5,4,3,2,1,0:T(2,128)(2,1)S(1)} fusion(bf16[4,8,48,2,2,64]{5,4,3,2,1,0:T(2,128)(2,1)S(1)} %copy-done.2, pred[4,8,48]{2,1,0:T(8,128)(4,1)S(1)} %iota_compare_fusion), kind=kLoop, calls=%fused_computation | loop fusion | flops 393216 | bytes 1574400 | tf_op jit(solution)/shard_map/convert_element_type | solution.py:38
  15.0 8.0 %constant_dynamic-slice_fusion = (bf16[4,8,48,2,1,64]{5,4,3,2,1,0:T(2,128)(2,1)S(1)}, f32[4,8,48,2,1,64]{5,4,3,2,1,0:T(1,128)S(1)}, f32[4,8,48,2,1,64]{5,4,3,2,1,0:T(1,128)}, bf16[4,8,48,2,1,64]{5,4,3,2,1,0:T(2,128)(2,1)}) fusion(bf16[4,8,48,2,2,64]{5,4,3,2,1,0:T(2,128)(2,1)S(1)} %select_convert_fusion, s32[]{:T(128)S(6)} %select_n.40, s32[]{:T(128)S(6)} %select_n.39, ...), kind=kLoop, calls=%fused_computation.44 | loop fusion | flops 393216 | bytes 3932168 | tf_op jit(solution)/shard_map/jit(dynamic_index_in_dim)/dynamic_slice | solution.py:59
  23.0 0.1 copy.131
  23.1 0.7 copy.94
  23.8 0.5 collective-permute-start.1
  24.3 1.9 %collective-permute-done.1 = bf16[4,8,48,2,64]{4,3,2,1,0:T(2,128)(2,1)S(1)} collective-permute-done((bf16[4,8,48,2,64]{4,3,2,1,0:T(2,128)(2,1)S(1)}, bf16[4,8,48,2,64]{4,3,2,1,0:T(2,128)(2,1)S(1)}, u32[]{:S(2)}, u32[]{:S(2)}) %collective-permute-start.1) | collective-permute-done | bytes 393248 | tf_op jit(solution)/shard_map/ppermute | solution.py:13
  26.2 0.8 add_convert_fusion
  27.1 0.1 copy.95
  27.2 0.3 broadcast_in_dim.32
  27.5 1.9 %reshape.161 = bf16[16,2,12288]{2,1,0:T(2,128)(2,1)} reshape(bf16[16,4,2,48,64]{4,3,2,1,0:T(8,128)(2,1)S(1)} %bitcast.73) | data formatting | bytes 1572864
  29.4 7.3 %all-to-all-start.1 = ((bf16[16,2,12288]{2,1,0:T(2,128)(2,1)}), bf16[16,2,12288]{2,1,0:T(2,128)(2,1)S(1)}, u32[]{:S(2)}, u32[]{:S(2)}) async-start(bf16[16,2,12288]{2,1,0:T(2,128)(2,1)} %reshape.161), calls=%async_computation.1 | async-start | bytes 1572864 | tf_op jit(solution)/shard_map/all_to_all | solution.py:63
  36.8 0.1 copy.132
  36.9 0.7 copy.80
  37.6 0.5 collective-permute-start
  38.1 1.9 %collective-permute-done = bf16[4,8,48,2,64]{4,3,2,1,0:T(2,128)(2,1)S(1)} collective-permute-done((bf16[4,8,48,2,64]{4,3,2,1,0:T(2,128)(2,1)S(1)}, bf16[4,8,48,2,64]{4,3,2,1,0:T(2,128)(2,1)S(1)}, u32[]{:S(2)}, u32[]{:S(2)}) %collective-permute-start) | collective-permute-done | bytes 393248 | tf_op jit(solution)/shard_map/ppermute | solution.py:13
  40.0 0.8 add_convert_fusion.1
  40.8 0.1 copy.81
  40.9 0.3 broadcast_in_dim.30
  41.3 1.9 %reshape.159 = bf16[16,2,12288]{2,1,0:T(2,128)(2,1)} reshape(bf16[16,4,2,48,64]{4,3,2,1,0:T(8,128)(2,1)S(1)} %bitcast.74) | data formatting | bytes 1572864
  43.2 12.3 %all-to-all-done.1 = bf16[16,2,12288]{2,1,0:T(2,128)(2,1)S(1)} async-done(((bf16[16,2,12288]{2,1,0:T(2,128)(2,1)}), bf16[16,2,12288]{2,1,0:T(2,128)(2,1)S(1)}, u32[]{:S(2)}, u32[]{:S(2)}) %all-to-all-start.1) | async-done | bytes 786464 | tf_op jit(solution)/shard_map/all_to_all | solution.py:63
  55.5 5.5 %all-to-all-start = ((bf16[16,2,12288]{2,1,0:T(2,128)(2,1)}), bf16[16,2,12288]{2,1,0:T(2,128)(2,1)S(1)}, u32[]{:S(2)}, u32[]{:S(2)}) async-start(bf16[16,2,12288]{2,1,0:T(2,128)(2,1)} %reshape.159), calls=%async_computation | async-start | bytes 1572864 | tf_op jit(solution)/shard_map/all_to_all | solution.py:63
  61.0 0.7 copy.97
  61.7 2.3 %copy.83 = bf16[4,2,128,384]{2,1,3,0:T(2,128)(2,1)S(1)} copy(bf16[4,2,128,384]{3,2,1,0:T(8,128)(2,1)} %param.8) | data formatting | bytes 1572864 | tf_op args[3]
  63.9 1.4 %reshape.154 = bf16[4,256,8,48,1,1]{1,3,2,0,4,5:T(8,128)(2,1)} reshape(bf16[4,2,128,384]{2,1,3,0:T(2,128)(2,1)S(1)} %copy.97) | data formatting | bytes 1572864 | tf_op jit(solution)/shard_map/reshape | solution.py:45
  65.3 1.4 %reshape.152 = bf16[4,256,8,48,1,1]{1,3,2,0,4,5:T(8,128)(2,1)} reshape(bf16[4,2,128,384]{2,1,3,0:T(2,128)(2,1)S(1)} %copy.83) | data formatting | bytes 1572864 | tf_op jit(solution)/shard_map/reshape | solution.py:45
  66.7 1.0 %reshape.162 = bf16[16,4,2,48,64]{4,3,2,1,0:T(8,128)(2,1)S(1)} reshape(bf16[16,2,12288]{2,1,0:T(2,128)(2,1)S(1)} %all-to-all-done.1) | data formatting | bytes 1572864
  67.8 1.7 %fusion.7 = f32[4,256,2,2,64]{1,4,3,2,0:T(8,128)S(1)} fusion(bf16[4,8,2,48,2,64]{5,3,4,0,2,1:T(8,128)(2,1)S(1)} %bitcast.75, bf16[4,256,8,48,1,1]{1,3,2,0,4,5:T(8,128)(2,1)} %reshape.154), kind=kOutput, calls=%fused_computation.13 | convolution fusion | flops 201326592 | bytes 2621440 | tf_op jit(solution)/shard_map/fnbk,fbgkcp->fngcp/dot_general | solution.py:46
  69.5 0.5 reshape.149
  70.1 1.1 %fusion.28 = (f32[4,1,128,2,1,64]{2,1,5,4,3,0:T(1,128)S(1)}, f32[4,1,128,2,1,64]{2,1,5,4,3,0:T(1,128)S(1)}, f32[4,1,128,2,1,64]{2,1,5,4,3,0:T(1,128)S(1)}, f32[4,1,128,2,1,64]{2,1,5,4,3,0:T(1,128)S(1)}) fusion(f32[4,2,128,2,2,64]{2,1,5,4,3,0:T(2,128)S(1)} %reshape.149), kind=kLoop, calls=%fused_computation.49 | loop fusion | bytes 2097152 | tf_op jit(solution)/shard_map/slice | solution.py:48
  71.3 0.9 copy.104
  72.1 7.5 %all-to-all-done = bf16[16,2,12288]{2,1,0:T(2,128)(2,1)S(1)} async-done(((bf16[16,2,12288]{2,1,0:T(2,128)(2,1)}), bf16[16,2,12288]{2,1,0:T(2,128)(2,1)S(1)}, u32[]{:S(2)}, u32[]{:S(2)}) %all-to-all-start) | async-done | bytes 786464 | tf_op jit(solution)/shard_map/all_to_all | solution.py:63
  79.7 1.0 %reshape.160 = bf16[16,4,2,48,64]{4,3,2,1,0:T(8,128)(2,1)S(1)} reshape(bf16[16,2,12288]{2,1,0:T(2,128)(2,1)S(1)} %all-to-all-done) | data formatting | bytes 1572864
  80.7 1.7 %fusion.4 = f32[4,256,2,2,64]{1,4,3,2,0:T(8,128)S(1)} fusion(bf16[4,8,2,48,2,64]{5,3,4,0,2,1:T(8,128)(2,1)S(1)} %bitcast.76, bf16[4,256,8,48,1,1]{1,3,2,0,4,5:T(8,128)(2,1)} %reshape.152), kind=kOutput, calls=%fused_computation.12 | convolution fusion | flops 201326592 | bytes 2621440 | tf_op jit(solution)/shard_map/fnbk,fbgkcp->fngcp/dot_general | solution.py:46
  82.4 0.5 reshape.143
  83.0 1.1 %fusion.29 = (f32[4,1,128,2,1,64]{2,1,5,4,3,0:T(1,128)S(1)}, f32[4,1,128,2,1,64]{2,1,5,4,3,0:T(1,128)S(1)}, f32[4,1,128,2,1,64]{2,1,5,4,3,0:T(1,128)S(1)}, f32[4,1,128,2,1,64]{2,1,5,4,3,0:T(1,128)S(1)}) fusion(f32[4,2,128,2,2,64]{2,1,5,4,3,0:T(2,128)S(1)} %reshape.143), kind=kLoop, calls=%fused_computation.50 | loop fusion | bytes 2097152 | tf_op jit(solution)/shard_map/slice | solution.py:48
  84.2 0.9 copy.103
  (22 shorter events, 0.5 us)
Async XLA Ops:
  4.7 1.0 %copy-start.5 = (bf16[4,128,256]{2,1,0:T(8,128)(2,1)S(1)}, bf16[4,128,256]{2,1,0:T(8,128)(2,1)}, u32[]{:S(2)}) copy-start(bf16[4,128,256]{2,1,0:T(8,128)(2,1)} %param.6) | copy-start | bytes 786436
  4.7 1.2 %copy-start.4 = (bf16[4,2,128,384]{3,2,1,0:T(8,128)(2,1)S(1)}, bf16[4,2,128,384]{3,2,1,0:T(8,128)(2,1)}, u32[]{:S(2)}) copy-start(bf16[4,2,128,384]{3,2,1,0:T(8,128)(2,1)} %param.8) | copy-start | bytes 2359300
  10.3 2.3 %copy-start.2 = (bf16[4,8,48,2,2,64]{5,4,3,2,1,0:T(2,128)(2,1)S(1)}, bf16[4,8,48,2,2,64]{5,4,3,2,1,0:T(2,128)(2,1)}, u32[]{:S(2)}) copy-start(bf16[4,8,48,2,2,64]{5,4,3,2,1,0:T(2,128)(2,1)} %reshape.145) | copy-start | bytes 2359300
  23.8 2.4 %collective-permute-start.1 = (bf16[4,8,48,2,64]{4,3,2,1,0:T(2,128)(2,1)S(1)}, bf16[4,8,48,2,64]{4,3,2,1,0:T(2,128)(2,1)S(1)}, u32[]{:S(2)}, u32[]{:S(2)}) collective-permute-start(bf16[4,8,48,2,64]{4,3,2,1,0:T(2,128)(2,1)S(1)} %copy.94), channel_id=1, source_target_pairs={{0,1},{1,0},{2,3},{3,2},{4,5},{5,4},{6,7},{7,6},{8,9},{9,8},{10,11... | collective-permute-start | bytes 1179656 | tf_op jit(solution)/shard_map/ppermute | solution.py:13
  27.5 9.2 %copy-start.1 = (bf16[4,8,48,2,1,64]{5,4,3,2,1,0:T(2,128)(2,1)S(1)}, bf16[4,8,48,2,1,64]{5,4,3,2,1,0:T(2,128)(2,1)}, u32[]{:S(2)}) copy-start(bf16[4,8,48,2,1,64]{5,4,3,2,1,0:T(2,128)(2,1)} %get-tuple-element.25) | copy-start | bytes 1179652
  29.4 26.0 %all-to-all-start.1 = ((bf16[16,2,12288]{2,1,0:T(2,128)(2,1)}), bf16[16,2,12288]{2,1,0:T(2,128)(2,1)S(1)}, u32[]{:S(2)}, u32[]{:S(2)}) async-start(bf16[16,2,12288]{2,1,0:T(2,128)(2,1)} %reshape.161), calls=%async_computation.1 | async-start | bytes 1572864 | tf_op jit(solution)/shard_map/all_to_all | solution.py:63
  36.8 3.2 %copy-start = (f32[4,8,48,2,1,64]{5,4,3,2,1,0:T(1,128)S(1)}, f32[4,8,48,2,1,64]{5,4,3,2,1,0:T(1,128)}, u32[]{:S(2)}) copy-start(f32[4,8,48,2,1,64]{5,4,3,2,1,0:T(1,128)} %get-tuple-element.24) | copy-start | bytes 2359300
  37.6 2.4 %collective-permute-start = (bf16[4,8,48,2,64]{4,3,2,1,0:T(2,128)(2,1)S(1)}, bf16[4,8,48,2,64]{4,3,2,1,0:T(2,128)(2,1)S(1)}, u32[]{:S(2)}, u32[]{:S(2)}) collective-permute-start(bf16[4,8,48,2,64]{4,3,2,1,0:T(2,128)(2,1)S(1)} %copy.80), channel_id=1, source_target_pairs={{0,1},{1,0},{2,3},{3,2},{4,5},{5,4},{6,7},{7,6},{8,9},{9,8},{10,11... | collective-permute-start | bytes 1179656 | tf_op jit(solution)/shard_map/ppermute | solution.py:13
  43.2 17.8 %copy-start.3 = (bf16[4,2,128,384]{3,2,1,0:T(8,128)(2,1)S(1)}, bf16[4,2,128,384]{3,2,1,0:T(8,128)(2,1)}, u32[]{:S(2)}) copy-start(bf16[4,2,128,384]{3,2,1,0:T(8,128)(2,1)} %param.7) | copy-start | bytes 2359300
  55.5 24.2 %all-to-all-start = ((bf16[16,2,12288]{2,1,0:T(2,128)(2,1)}), bf16[16,2,12288]{2,1,0:T(2,128)(2,1)S(1)}, u32[]{:S(2)}, u32[]{:S(2)}) async-start(bf16[16,2,12288]{2,1,0:T(2,128)(2,1)} %reshape.159), calls=%async_computation | async-start | bytes 1572864 | tf_op jit(solution)/shard_map/all_to_all | solution.py:63
where the time goes:
time: 85.7 us; the launch traced here: 85.1 us
  local copies, waits for them, and re-layouts  24.8 us (29%)
  waiting for transfers between devices  23.6 us (28%)
  other arithmetic  15.5 us (18%)
  starting transfers between devices  13.8 us (16%)
  matrix products  6.38 us (7%)
  between operations  1.01 us (1%)
    all_to_all x2, waiting for transfers between devices, carry_over(): lax.all_to_all(outgoing, 'col', split_axis=1, concat_axis=1, tiled=True)  19.8 us
    all_to_all x2, starting transfers between devices, carry_over(): lax.all_to_all(outgoing, 'col', split_axis=1, concat_axis=1, tiled=True)  12.8 us
    unnamed x22, local copies, waits for them, and re-layouts  12 us
    dynamic_slice x1, other arithmetic, carry_over(): lax.dynamic_index_in_dim(halves, 1 - my_side, axis=4, keepdims=False)  8.03 us
    convert_element_type x2, other arithmetic, partials(): jnp.where(alive_mask[:, :, :, None, None], coeffs, 0.0).astype(jnp.bfloat16)  4.64 us
    ppermute x2, waiting for transfers between devices, swapped(): lax.ppermute(value, axis, [(i, i ^ 1 << stride) for i in range(lax.axis_s...  3.82 us
    dot_general x2, matrix products, apply_split(): jnp.einsum('fnbk,fbgkcp->fngcp', stacked, summed, preferred_element_type=...  3.49 us
    dot_general x2, matrix products, partials(): jnp.einsum('fnq,fnc->fqc', stacked, operand, preferred_element_type=jnp.f...  2.89 us
  transfers between devices with their start and end apart: 4, of which 4 were waited for; matrix products, arithmetic and copies ran while one was open for 18% of the time, Pallas kernels for 0%

commit v1 on v0

v1 whole, which is shorter than its diff:
```python
import jax
import jax.numpy as jnp
from jax import lax
from jax.experimental import pallas as pl
from jax.experimental.pallas import tpu as pltpu
from jax.sharding import PartitionSpec as P

RANKS = (8, 16, 32, 48)
CORES = 2
GROUP = 384
VMEM_LIMIT = 56 * 1024 * 1024


def flipped(index, step, count):
    if count & (count - 1):
        return (index + step) % count
    out = index
    bit = 1
    while bit < count:
        if step & bit:
            out = out + (1 - 2 * ((index // bit) % 2)) * bit
        bit *= 2
    return out


def partner_steps(count):
    steps = []
    top = count // 2
    while top >= 1:
        steps += list(range(top, min(2 * top, count)))
        top //= 2
    return steps if not count & (count - 1) else list(range(1, count))


def kernel(
    class_ref, x_ref, r_ref, v_ref, u_ref, fwd_ref, adj_ref,
    v_all, u_all, x_all, r_all, coeff, got, result,
    in_sem, in_send, in_recv, send_sem, recv_sem, out_sem, out_send, out_recv,
):
    freqs, _, half_rows, width = v_ref.shape
    tiles = class_ref.shape[1]
    rank = width // tiles
    points = x_ref.shape[2] // 2
    own = freqs // CORES
    index = lax.axis_index("col")
    tile = index // CORES
    side = index % CORES
    sibling = tile * CORES + 1 - side
    first = side * own
    other_first = (1 - side) * own
    steps = partner_steps(tiles)

    loads = ((v_ref, v_all), (x_ref, x_all), (u_ref, u_all), (r_ref, r_all))

    def local_load(a, f):
        src, dst = loads[a]
        return pltpu.make_async_copy(src.at[first + f], dst.at[f, side], in_sem.at[a, f])

    def remote_load(a, f):
        src, dst = loads[a]
        return pltpu.make_async_remote_copy(
            src_ref=src.at[other_first + f], dst_ref=dst.at[f, side],
            send_sem=in_send.at[a, f], recv_sem=in_recv.at[a, f],
            device_id={"col": sibling}, device_id_type=pl.DeviceIdType.MESH,
        )

    pairs = [(d, f) for d in range(2) for f in range(own)]
    for d, f in pairs:
        local_load(2 * d, f).start()
        local_load(2 * d + 1, f).start()

    barrier = pltpu.get_barrier_semaphore()
    pl.semaphore_signal(barrier, inc=1, device_id={"col": sibling}, device_id_type=pl.DeviceIdType.MESH)
    for step in steps:
        peer = flipped(tile, step, tiles) * CORES + side
        pl.semaphore_signal(barrier, inc=1, device_id={"col": peer}, device_id_type=pl.DeviceIdType.MESH)
    pl.semaphore_wait(barrier, tiles)

    for d, f in pairs:
        remote_load(2 * d, f).start()
        remote_load(2 * d + 1, f).start()

    def send(d, f, step):
        peer = flipped(tile, step, tiles)
        return pltpu.make_async_remote_copy(
            src_ref=coeff.at[d, f, peer], dst_ref=got.at[d, f, tile],
            send_sem=send_sem.at[d, f, step], recv_sem=recv_sem.at[d, f, step],
            device_id={"col": peer * CORES + side}, device_id_type=pl.DeviceIdType.MESH,
        )

    row = lax.broadcasted_iota(jnp.int32, (rank, 2 * points), 0)
    for d, f in pairs:
        factor, field = ((v_all, x_all), (u_all, r_all))[d]
        for a in (2 * d, 2 * d + 1):
            local_load(a, f).wait()
            remote_load(a, f).wait_recv()
        parts = []
        for half in range(CORES):
            block = field[f, half]
            parts += [block, jnp.concatenate([block[:, points:], -block[:, :points]], axis=1)]
        operand = jnp.concatenate(parts, axis=0)
        group = GROUP if width % GROUP == 0 else width
        for g in range(width // group):
            stacked = factor[f, :, :, :, g * group:(g + 1) * group]
            stacked = stacked.reshape(2 * CORES * half_rows, group)
            sums = lax.dot_general(
                stacked, operand, (((0,), (0,)), ((), ())), preferred_element_type=jnp.float32)
            for k in range(group // rank):
                to = g * (group // rank) + k
                cls = class_ref[first + f, to, tile] if d == 0 else class_ref[first + f, tile, to]
                alive = jnp.where(cls == 0, RANKS[0], jnp.where(
                    cls == 1, RANKS[1], jnp.where(cls == 2, RANKS[2], RANKS[3])))
                kept = jnp.where(row < alive, sums[k * rank:(k + 1) * rank], 0.0)
                coeff[d, f, to] = kept.astype(jnp.bfloat16)
        for step in steps:
            send(d, f, step).start()

    def outputs(d, f):
        out = (fwd_ref, adj_ref)[d]
        local = pltpu.make_async_copy(result.at[d, f, side], out.at[first + f], out_sem.at[d, f])
        remote = pltpu.make_async_remote_copy(
            src_ref=result.at[d, f, 1 - side], dst_ref=out.at[first + f],
            send_sem=out_send.at[d, f], recv_sem=out_recv.at[d, f],
            device_id={"col": sibling}, device_id_type=pl.DeviceIdType.MESH,
        )
        return local, remote

    for d, f in pairs:
        factor = (u_all, v_all)[d]
        got[d, f, tile] = coeff[d, f, tile]
        for step in steps:
            send(d, f, step).wait_recv()
        values = got[d, f].reshape(width, 2 * points)
        turned = jnp.concatenate([-values[:, points:], values[:, :points]], axis=1)
        real_rows = factor[f, :, 0].reshape(CORES * half_rows, width)
        imag_rows = factor[f, :, 1].reshape(CORES * half_rows, width)
        total = jnp.dot(real_rows, values, preferred_element_type=jnp.float32)
        total = total + jnp.dot(imag_rows, turned, preferred_element_type=jnp.float32)
        result[d, f] = total.astype(jnp.bfloat16).reshape(CORES, half_rows, 2 * points)
        local, remote = outputs(d, f)
        remote.start()
        local.start()

    for d, f in pairs:
        for a in (2 * d, 2 * d + 1):
            remote_load(a, f).wait_send()
        for step in steps:
            send(d, f, step).wait_send()
        local, remote = outputs(d, f)
        local.wait()
        remote.wait()


def body(sources_field, residual_field, v_factors, u_factors, tile_class):
    freqs, _, half_rows, width = v_factors.shape
    tiles = tile_class.shape[1]
    points2 = sources_field.shape[2]
    own = freqs // CORES
    steps = max(tiles, 2)
    any_spec = pl.BlockSpec(memory_space=pl.ANY)
    dma = pltpu.SemaphoreType.DMA
    bf16 = jnp.bfloat16
    out = jax.ShapeDtypeStruct(sources_field.shape, bf16)
    flops = 2 * 2 * 2 * freqs * 2 * half_rows * width * points2
    return pl.pallas_call(
        kernel,
        out_shape=(out, out),
        in_specs=[pl.BlockSpec(memory_space=pltpu.SMEM)] + [any_spec] * 4,
        out_specs=(any_spec, any_spec),
        scratch_shapes=[
            pltpu.VMEM((own, CORES, 2, half_rows, width), bf16),
            pltpu.VMEM((own, CORES, 2, half_rows, width), bf16),
            pltpu.VMEM((own, CORES, half_rows, points2), bf16),
            pltpu.VMEM((own, CORES, half_rows, points2), bf16),
            pltpu.VMEM((2, own, tiles, width // tiles, points2), bf16),
            pltpu.VMEM((2, own, tiles, width // tiles, points2), bf16),
            pltpu.VMEM((2, own, CORES, half_rows, points2), bf16),
            dma((4, own)), dma((4, own)), dma((4, own)),
            dma((2, own, steps)), dma((2, own, steps)),
            dma((2, own)), dma((2, own)), dma((2, own)),
        ],
        compiler_params=pltpu.CompilerParams(
            collective_id=0, has_side_effects=True, vmem_limit_bytes=VMEM_LIMIT),
        cost_estimate=pl.CostEstimate(
            flops=flops, transcendentals=0, bytes_accessed=4 * v_factors.size + 8 * sources_field.size),
    )(tile_class, sources_field, residual_field, v_factors, u_factors)


def solution(mesh):
    placed = (
        P("patch", "col", None),
        P("patch", "col", None),
        P("patch", None, "col", None),
        P("patch", None, "col", None),
        P("patch", None, None),
    )
    return jax.shard_map(
        body,
        mesh=mesh,
        in_specs=placed,
        out_specs=(P("patch", "col", None), P("patch", "col", None)),
        check_vma=False,
    )
```

time: 85.7 us -> 31.7 us (0.37)
  Pallas kernels: 0 us -> 28.4 us
  waiting for transfers between devices: 23.6 us -> 0 us
  local copies, waits for them, and re-layouts: 24.8 us -> 2.42 us
  other arithmetic: 15.5 us -> 0 us
  starting transfers between devices: 13.8 us -> 0 us
  matrix products: 6.38 us -> 0 us
    pallas_call x0 -> x1, Pallas kernels: none -> 28.4 us  [body(): pl.pallas_call(kernel, out_shape=(out, out), in_specs=[pl.BlockSpec(memor...]
    all_to_all x2 -> x0, waiting for transfers between devices: 19.8 us -> none  [carry_over(): lax.all_to_all(outgoing, 'col', split_axis=1, concat_axis=1, tiled=True)]
    all_to_all x2 -> x0, starting transfers between devices: 12.8 us -> none  [carry_over(): lax.all_to_all(outgoing, 'col', split_axis=1, concat_axis=1, tiled=True)]
    unnamed x22 -> x4, local copies, waits for them, and re-layouts: 12 us -> 2.42 us
    dynamic_slice x1 -> x0, other arithmetic: 8.03 us -> none  [carry_over(): lax.dynamic_index_in_dim(halves, 1 - my_side, axis=4, keepdims=False)]
    dot_general x4 -> x0, matrix products: 6.38 us -> none  [the longest x2 3.49 us: apply_split(): jnp.einsum('fnbk,fbgkcp->fngcp', stacked, summed, preferred_element_type=...]
    convert_element_type x4 -> x0, other arithmetic: 6.3 us -> none  [the longest x2 4.64 us: partials(): jnp.where(alive_mask[:, :, :, None, None], coeffs, 0.0).astype(jnp.bfloat16)]
    reshape x6 -> x0, local copies, waits for them, and re-layouts: 6.17 us -> none  [the longest x2 2.81 us: apply_split(): target_factor.reshape(freq_count, 2 * half_rows, tile_count, rank_width)]
  transfers between devices with their start and end apart: 4 -> 0, of which waited for: 4 -> 0; matrix products, arithmetic and copies ran while one was open for 18% -> 0% of each run, Pallas kernels for 0% -> 0%
where the time goes in v1:
time: 31.7 us; the launch traced here: 31.5 us
  Pallas kernels  28.4 us (90%)
  local copies, waits for them, and re-layouts  2.42 us (8%)
  between operations  0.65 us (2%)
    pallas_call x1, Pallas kernels, body(): pl.pallas_call(kernel, out_shape=(out, out), in_specs=[pl.BlockSpec(memor...  28.4 us
    unnamed x4, local copies, waits for them, and re-layouts  2.42 us

profile of v1, /device:TPU:0, one launch (start us, length us, event | category | flops | bytes accessed | tf_op | source)
XLA Modules:
  0.0 31.5 jit_solution(7587454314499259321)
XLA Ops:
  0.6 28.4 %shard_map.68 = (bf16[4,128,256]{2,1,0:T(8,128)(2,1)}, bf16[4,128,256]{2,1,0:T(8,128)(2,1)}) custom-call(s32[4,8,8]{2,1,0:T(8,128)} %class_ref.1, bf16[4,128,256]{2,1,0:T(8,128)(2,1)} %x_ref.1, bf16[4,128,256]{2,1,0:T(8,128)(2,1)} %r_ref.1, bf16[4,2,128,384]{3,2,1,0:T(8,128)(2,1)} %v_ref.1, bf16[4,2,128,384]{3,2,1,0:T(8,128)(2,1)} %u_ref.1), custom_call_target="tpu_custom_call" | custom-call | flops 805306368 | bytes 2621440 | tf_op jit(solution)/shard_map/pallas_call | solution.py:165
  29.1 0.0 copy-start
  29.1 1.7 %copy.9 = bf16[4,128,256]{2,1,0:T(8,128)(2,1)} copy(bf16[4,128,256]{2,1,0:T(8,128)(2,1)} %get-tuple-element.4) | data formatting | bytes 524288
  30.8 0.0 copy-done
  30.8 0.7 %copy.10 = bf16[4,128,256]{2,1,0:T(8,128)(2,1)} copy(bf16[4,128,256]{2,1,0:T(8,128)(2,1)S(1)} %copy-done) | data formatting | bytes 524288
Async XLA Ops:
  29.1 1.7 %copy-start = (bf16[4,128,256]{2,1,0:T(8,128)(2,1)S(1)}, bf16[4,128,256]{2,1,0:T(8,128)(2,1)}, u32[]{:S(2)}) copy-start(bf16[4,128,256]{2,1,0:T(8,128)(2,1)} %get-tuple-element.5) | copy-start | bytes 786436

commit v2 on v1

--- a/solution.py
+++ b/solution.py
@@ -35,7 +35,7 @@
 def kernel(
     class_ref, x_ref, r_ref, v_ref, u_ref, fwd_ref, adj_ref,
     v_all, u_all, x_all, r_all, coeff, got, result,
-    in_sem, in_send, in_recv, send_sem, recv_sem, out_sem, out_send, out_recv,
+    in_sem, in_send, in_recv, send_sem, recv_sem, out_send, out_recv,
 ):
     freqs, _, half_rows, width = v_ref.shape
     tiles = class_ref.shape[1]
@@ -115,15 +115,12 @@
         for step in steps:
             send(d, f, step).start()
 
-    def outputs(d, f):
-        out = (fwd_ref, adj_ref)[d]
-        local = pltpu.make_async_copy(result.at[d, f, side], out.at[first + f], out_sem.at[d, f])
-        remote = pltpu.make_async_remote_copy(
-            src_ref=result.at[d, f, 1 - side], dst_ref=out.at[first + f],
+    def output(d, f):
+        return pltpu.make_async_remote_copy(
+            src_ref=result.at[d, f, 1 - side], dst_ref=(fwd_ref, adj_ref)[d].at[first + f],
             send_sem=out_send.at[d, f], recv_sem=out_recv.at[d, f],
             device_id={"col": sibling}, device_id_type=pl.DeviceIdType.MESH,
         )
-        return local, remote
 
     for d, f in pairs:
         factor = (u_all, v_all)[d]
@@ -137,18 +134,27 @@
         total = jnp.dot(real_rows, values, preferred_element_type=jnp.float32)
         total = total + jnp.dot(imag_rows, turned, preferred_element_type=jnp.float32)
         result[d, f] = total.astype(jnp.bfloat16).reshape(CORES, half_rows, 2 * points)
-        local, remote = outputs(d, f)
-        remote.start()
-        local.start()
+        output(d, f).start()
+        (fwd_ref, adj_ref)[d][first + f] = result[d, f, side]
 
     for d, f in pairs:
         for a in (2 * d, 2 * d + 1):
             remote_load(a, f).wait_send()
         for step in steps:
             send(d, f, step).wait_send()
-        local, remote = outputs(d, f)
-        local.wait()
-        remote.wait()
+        output(d, f).wait()
+
+
+def copy_out(*refs):
+    srcs, dsts, sem = refs[:2], refs[2:4], refs[4]
+    copies = [
+        pltpu.make_async_copy(src.at[f], dst.at[f], sem.at[n, f])
+        for n, (src, dst) in enumerate(zip(srcs, dsts)) for f in range(src.shape[0])
+    ]
+    for copy in copies:
+        copy.start()
+    for copy in copies:
+        copy.wait()
 
 
 def body(sources_field, residual_field, v_factors, u_factors, tile_class):
@@ -162,11 +168,11 @@
     bf16 = jnp.bfloat16
     out = jax.ShapeDtypeStruct(sources_field.shape, bf16)
     flops = 2 * 2 * 2 * freqs * 2 * half_rows * width * points2
-    return pl.pallas_call(
+    fields = pl.pallas_call(
         kernel,
-        out_shape=(out, out),
-        in_specs=[pl.BlockSpec(memory_space=pltpu.SMEM)] + [any_spec] * 4,
-        out_specs=(any_spec, any_spec),
+        out_shape=(pltpu.VMEM(out.shape, bf16), pltpu.VMEM(out.shape, bf16)),
+        in_specs=[pl.BlockSpec(memory_space=pltpu.SMEM)] + [pl.BlockSpec(memory_space=pltpu.HBM)] * 4,
+        out_specs=(pl.BlockSpec(memory_space=pltpu.VMEM),) * 2,
         scratch_shapes=[
             pltpu.VMEM((own, CORES, 2, half_rows, width), bf16),
             pltpu.VMEM((own, CORES, 2, half_rows, width), bf16),
@@ -177,13 +183,21 @@
             pltpu.VMEM((2, own, CORES, half_rows, points2), bf16),
             dma((4, own)), dma((4, own)), dma((4, own)),
             dma((2, own, steps)), dma((2, own, steps)),
-            dma((2, own)), dma((2, own)), dma((2, own)),
+            dma((2, own)), dma((2, own)),
         ],
         compiler_params=pltpu.CompilerParams(
             collective_id=0, has_side_effects=True, vmem_limit_bytes=VMEM_LIMIT),
         cost_estimate=pl.CostEstimate(
             flops=flops, transcendentals=0, bytes_accessed=4 * v_factors.size + 8 * sources_field.size),
     )(tile_class, sources_field, residual_field, v_factors, u_factors)
+    return pl.pallas_call(
+        copy_out,
+        out_shape=(out, out),
+        in_specs=[pl.BlockSpec(memory_space=pltpu.VMEM)] * 2,
+        out_specs=(any_spec, any_spec),
+        scratch_shapes=[dma((2, freqs))],
+        compiler_params=pltpu.CompilerParams(vmem_limit_bytes=4 * 1024 * 1024),
+    )(*fields)
 
 
 def solution(mesh):

time: 31.7 us -> 30 us (0.946)
  local copies, waits for them, and re-layouts: 2.42 us -> 0 us
  Pallas kernels: 28.4 us -> 29.1 us
    unnamed x4 -> x0, local copies, waits for them, and re-layouts: 2.42 us -> none
    pallas_call x1 -> x2, Pallas kernels: 28.4 us -> 29.1 us  [the longest x1 28.3 us: body(): pl.pallas_call(kernel, out_shape=(pltpu.VMEM(out.shape, bf16), pltpu.VMEM...]
where the time goes in v2:
time: 30 us; the launch traced here: 29.8 us
  Pallas kernels  29.1 us (97%)
  between operations  0.64 us (2%)
    pallas_call x1, Pallas kernels, body(): pl.pallas_call(kernel, out_shape=(pltpu.VMEM(out.shape, bf16), pltpu.VMEM...  28.3 us
    pallas_call x1, Pallas kernels, body(): pl.pallas_call(copy_out, out_shape=(out, out), in_specs=[pl.BlockSpec(mem...  0.85 us

profile of v2, /device:TPU:0, one launch (start us, length us, event | category | flops | bytes accessed | tf_op | source)
XLA Modules:
  0.0 29.8 jit_solution(17157647957937649712)
XLA Ops:
  0.6 28.3 %shard_map.68 = (bf16[4,128,256]{2,1,0:T(8,128)(2,1)S(1)}, bf16[4,128,256]{2,1,0:T(8,128)(2,1)S(1)}) custom-call(s32[4,8,8]{2,1,0:T(8,128)} %class_ref.1, bf16[4,128,256]{2,1,0:T(8,128)(2,1)} %x_ref.1, bf16[4,128,256]{2,1,0:T(8,128)(2,1)} %r_ref.1, bf16[4,2,128,384]{3,2,1,0:T(8,128)(2,1)} %v_ref.1, bf16[4,2,128,384]{3,2,1,0:T(8,128)(2,1)} %u_ref.1), custom_call_target="tpu_custom_call" | custom-call | flops 805306368 | bytes 2621440 | tf_op jit(solution)/shard_map/pallas_call | solution.py:171
  28.9 0.9 %shard_map.69 = (bf16[4,128,256]{2,1,0:T(8,128)(2,1)}, bf16[4,128,256]{2,1,0:T(8,128)(2,1)}) custom-call(bf16[4,128,256]{2,1,0:T(8,128)(2,1)S(1)} %get-tuple-element.4.refs_0_, bf16[4,128,256]{2,1,0:T(8,128)(2,1)S(1)} %get-tuple-element.5.refs_1_), custom_call_target="tpu_custom_call" | custom-call | tf_op jit(solution)/shard_map/pallas_call | solution.py:193

commit v3 on v2

--- a/solution.py
+++ b/solution.py
@@ -9,33 +9,19 @@
 CORES = 2
 GROUP = 384
 VMEM_LIMIT = 56 * 1024 * 1024
-
-
-def flipped(index, step, count):
-    if count & (count - 1):
-        return (index + step) % count
-    out = index
-    bit = 1
-    while bit < count:
-        if step & bit:
-            out = out + (1 - 2 * ((index // bit) % 2)) * bit
-        bit *= 2
-    return out
-
-
-def partner_steps(count):
-    steps = []
-    top = count // 2
-    while top >= 1:
-        steps += list(range(top, min(2 * top, count)))
-        top //= 2
-    return steps if not count & (count - 1) else list(range(1, count))
+MESH = pl.DeviceIdType.MESH
+THROUGH = 2
+
+
+def packed_rows(tiles):
+    return tiles // 8 * RANKS[3] + tiles // 4 * RANKS[2] + tiles // 8 * RANKS[1]
 
 
 def kernel(
     class_ref, x_ref, r_ref, v_ref, u_ref, fwd_ref, adj_ref,
-    v_all, u_all, x_all, r_all, coeff, got, result,
-    in_sem, in_send, in_recv, send_sem, recv_sem, out_send, out_recv,
+    v_all, u_all, x_all, r_all, coeff, packed, landed, relayed, got, result,
+    in_sem, in_send, in_recv, near_send, far_send, got_recv, pack_send, pack_recv, relay_send,
+    out_send, out_recv,
 ):
     freqs, _, half_rows, width = v_ref.shape
     tiles = class_ref.shape[1]
@@ -48,7 +34,16 @@
     sibling = tile * CORES + 1 - side
     first = side * own
     other_first = (1 - side) * own
-    steps = partner_steps(tiles)
+    group = tiles // 2
+    inner = tiles // 4
+    upper = tile // group
+    place = tile % group
+    near_base = upper * group
+    far_base = (1 - upper) * group
+    lane = place % inner
+    gate = far_base + lane + upper * (group - inner)
+    slot_out = place // inner
+    is_gate = (place // inner) == (1 - upper)
 
     loads = ((v_ref, v_all), (x_ref, x_all), (u_ref, u_all), (r_ref, r_all))
 
@@ -61,32 +56,84 @@
         return pltpu.make_async_remote_copy(
             src_ref=src.at[other_first + f], dst_ref=dst.at[f, side],
             send_sem=in_send.at[a, f], recv_sem=in_recv.at[a, f],
-            device_id={"col": sibling}, device_id_type=pl.DeviceIdType.MESH,
+            device_id={"col": sibling}, device_id_type=MESH,
         )
 
     pairs = [(d, f) for d in range(2) for f in range(own)]
+    through = pairs[:THROUGH]
     for d, f in pairs:
         local_load(2 * d, f).start()
         local_load(2 * d + 1, f).start()
 
     barrier = pltpu.get_barrier_semaphore()
-    pl.semaphore_signal(barrier, inc=1, device_id={"col": sibling}, device_id_type=pl.DeviceIdType.MESH)
-    for step in steps:
-        peer = flipped(tile, step, tiles) * CORES + side
-        pl.semaphore_signal(barrier, inc=1, device_id={"col": peer}, device_id_type=pl.DeviceIdType.MESH)
+    pl.semaphore_signal(barrier, inc=1, device_id={"col": sibling}, device_id_type=MESH)
+    for step in range(1, tiles):
+        peer = ((tile + step) % tiles) * CORES + side
+        pl.semaphore_signal(barrier, inc=1, device_id={"col": peer}, device_id_type=MESH)
     pl.semaphore_wait(barrier, tiles)
 
     for d, f in pairs:
         remote_load(2 * d, f).start()
         remote_load(2 * d + 1, f).start()
 
-    def send(d, f, step):
-        peer = flipped(tile, step, tiles)
-        return pltpu.make_async_remote_copy(
-            src_ref=coeff.at[d, f, peer], dst_ref=got.at[d, f, tile],
-            send_sem=send_sem.at[d, f, step], recv_sem=recv_sem.at[d, f, step],
-            device_id={"col": peer * CORES + side}, device_id_type=pl.DeviceIdType.MESH,
-        )
+    def live(d, f, source, target):
+        cls = class_ref[first + f, target, source] if d == 0 else class_ref[first + f, source, target]
+        return jnp.where(cls == 0, RANKS[0], jnp.where(
+            cls == 1, RANKS[1], jnp.where(cls == 2, RANKS[2], RANKS[3])))
+
+    pack_rows = packed.shape[2]
+
+    def selection(d, f, source, base):
+        col = lax.broadcasted_iota(jnp.int32, (1, group * rank), 1)
+        spot = jnp.full((1, group * rank), -1, jnp.int32)
+        start = jnp.int32(0)
+        for q in range(group):
+            alive = live(d, f, source, base + q)
+            inside = (col >= q * rank) & (col < q * rank + alive)
+            spot = jnp.where(inside, col + (start - q * rank), spot)
+            start = start + alive
+        rows = lax.broadcasted_iota(jnp.int32, (pack_rows, group * rank), 0)
+        return jnp.where(rows == spot, 1.0, 0.0).astype(jnp.bfloat16)
+
+    def pack_copy(d, f):
+        return pltpu.make_async_remote_copy(
+            src_ref=packed.at[d, f], dst_ref=landed.at[d, f, slot_out],
+            send_sem=pack_send.at[d, f], recv_sem=pack_recv.at[d, f, slot_out],
+            device_id={"col": gate * CORES + side}, device_id_type=MESH)
+
+    def pack_wait(d, f, slot):
+        return pltpu.make_async_remote_copy(
+            src_ref=packed.at[d, f], dst_ref=landed.at[d, f, slot],
+            send_sem=pack_send.at[d, f], recv_sem=pack_recv.at[d, f, slot],
+            device_id={"col": gate * CORES + side}, device_id_type=MESH)
+
+    def near_copy(d, f, step):
+        q = (place + step) % group
+        return pltpu.make_async_remote_copy(
+            src_ref=coeff.at[d, f, near_base + q], dst_ref=got.at[d, f, tile],
+            send_sem=near_send.at[d, f, step], recv_sem=got_recv.at[d, f, tile],
+            device_id={"col": (near_base + q) * CORES + side}, device_id_type=MESH)
+
+    def relay_copy(d, f, slot, step):
+        q = (place + step) % group
+        source = far_base + slot * inner + lane
+        return pltpu.make_async_remote_copy(
+            src_ref=relayed.at[d, f, slot, q], dst_ref=got.at[d, f, source],
+            send_sem=relay_send.at[d, f, slot, step], recv_sem=got_recv.at[d, f, source],
+            device_id={"col": (near_base + q) * CORES + side}, device_id_type=MESH)
+
+    def got_wait(d, f, source):
+        pltpu.make_async_remote_copy(
+            src_ref=coeff.at[d, f, source], dst_ref=got.at[d, f, source],
+            send_sem=near_send.at[d, f, 0], recv_sem=got_recv.at[d, f, source],
+            device_id={"col": sibling}, device_id_type=MESH).wait_recv()
+
+    def far_copy(d, f, step):
+        q = (place + step) % group
+        return pltpu.make_async_remote_copy(
+            src_ref=coeff.at[d, f, far_base + q], dst_ref=got.at[d, f, tile],
+            send_sem=far_send.at[d, f, step], recv_sem=got_recv.at[d, f, tile],
+            device_id={"col": (far_base + q) * CORES + side}, device_id_type=MESH)
 
     row = lax.broadcasted_iota(jnp.int32, (rank, 2 * points), 0)
     for d, f in pairs:
@@ -99,34 +146,68 @@
             block = field[f, half]
             parts += [block, jnp.concatenate([block[:, points:], -block[:, :points]], axis=1)]
         operand = jnp.concatenate(parts, axis=0)
-        group = GROUP if width % GROUP == 0 else width
-        for g in range(width // group):
-            stacked = factor[f, :, :, :, g * group:(g + 1) * group]
-            stacked = stacked.reshape(2 * CORES * half_rows, group)
+        wide = GROUP if width % GROUP == 0 else width
+        for g in range(width // wide):
+            stacked = factor[f, :, :, :, g * wide:(g + 1) * wide]
+            stacked = stacked.reshape(2 * CORES * half_rows, wide)
             sums = lax.dot_general(
                 stacked, operand, (((0,), (0,)), ((), ())), preferred_element_type=jnp.float32)
-            for k in range(group // rank):
-                to = g * (group // rank) + k
-                cls = class_ref[first + f, to, tile] if d == 0 else class_ref[first + f, tile, to]
-                alive = jnp.where(cls == 0, RANKS[0], jnp.where(
-                    cls == 1, RANKS[1], jnp.where(cls == 2, RANKS[2], RANKS[3])))
+            for k in range(wide // rank):
+                to = g * (wide // rank) + k
+                alive = live(d, f, tile, to)
                 kept = jnp.where(row < alive, sums[k * rank:(k + 1) * rank], 0.0)
                 coeff[d, f, to] = kept.astype(jnp.bfloat16)
-        for step in steps:
-            send(d, f, step).start()
+        for step in range(1, group):
+            near_copy(d, f, step).start()
+        if (d, f) in through:
+            far = coeff[d, f, pl.ds(far_base, group)].reshape(group * rank, 2 * points)
+            packed[d, f] = jnp.dot(
+                selection(d, f, tile, far_base), far,
+                preferred_element_type=jnp.float32).astype(jnp.bfloat16)
+            pack_copy(d, f).start()
+        else:
+            for step in range(group):
+                far_copy(d, f, step).start()
+
+    def relay(d, f):
+        @pl.when(is_gate)
+        def _():
+            for slot in range(CORES):
+                source = far_base + slot * inner + lane
+                pack_wait(d, f, slot).wait_recv()
+                full = lax.dot_general(
+                    selection(d, f, source, near_base), landed[d, f, slot],
+                    (((0,), (0,)), ((), ())), preferred_element_type=jnp.float32)
+                relayed[d, f, slot] = full.astype(jnp.bfloat16).reshape(group, rank, 2 * points)
+                for step in range(1, group):
+                    relay_copy(d, f, slot, step).start()
+                got[d, f, source] = relayed[d, f, slot, place]
 
     def output(d, f):
         return pltpu.make_async_remote_copy(
             src_ref=result.at[d, f, 1 - side], dst_ref=(fwd_ref, adj_ref)[d].at[first + f],
             send_sem=out_send.at[d, f], recv_sem=out_recv.at[d, f],
-            device_id={"col": sibling}, device_id_type=pl.DeviceIdType.MESH,
+            device_id={"col": sibling}, device_id_type=MESH,
         )
+
+    for d, f in through:
+        relay(d, f)
 
     for d, f in pairs:
         factor = (u_all, v_all)[d]
         got[d, f, tile] = coeff[d, f, tile]
-        for step in steps:
-            send(d, f, step).wait_recv()
+        for step in range(1, group):
+            got_wait(d, f, near_base + (place + step) % group)
+        for slot in range(CORES):
+            for at in range(inner):
+                source = far_base + slot * inner + at
+                if (d, f) not in through:
+                    got_wait(d, f, source)
+                    continue
+
+                @pl.when(jnp.logical_not(is_gate & (lane == at)))
+                def _():
+                    got_wait(d, f, source)
         values = got[d, f].reshape(width, 2 * points)
         turned = jnp.concatenate([-values[:, points:], values[:, :points]], axis=1)
         real_rows = factor[f, :, 0].reshape(CORES * half_rows, width)
@@ -140,8 +221,19 @@
     for d, f in pairs:
         for a in (2 * d, 2 * d + 1):
             remote_load(a, f).wait_send()
-        for step in steps:
-            send(d, f, step).wait_send()
+        for step in range(1, group):
+            near_copy(d, f, step).wait_send()
+        if (d, f) in through:
+            pack_copy(d, f).wait_send()
+
+            @pl.when(is_gate)
+            def _():
+                for slot in range(CORES):
+                    for step in range(1, group):
+                        relay_copy(d, f, slot, step).wait_send()
+        else:
+            for step in range(group):
+                far_copy(d, f, step).wait_send()
         output(d, f).wait()
 
 
@@ -162,7 +254,9 @@
     tiles = tile_class.shape[1]
     points2 = sources_field.shape[2]
     own = freqs // CORES
-    steps = max(tiles, 2)
+    rank = width // tiles
+    group = tiles // 2
+    pack = packed_rows(tiles)
     any_spec = pl.BlockSpec(memory_space=pl.ANY)
     dma = pltpu.SemaphoreType.DMA
     bf16 = jnp.bfloat16
@@ -178,11 +272,15 @@
             pltpu.VMEM((own, CORES, 2, half_rows, width), bf16),
             pltpu.VMEM((own, CORES, half_rows, points2), bf16),
             pltpu.VMEM((own, CORES, half_rows, points2), bf16),
-            pltpu.VMEM((2, own, tiles, width // tiles, points2), bf16),
-            pltpu.VMEM((2, own, tiles, width // tiles, points2), bf16),
+            pltpu.VMEM((2, own, tiles, rank, points2), bf16),
+            pltpu.VMEM((2, own, pack, points2), bf16),
+            pltpu.VMEM((2, own, CORES, pack, points2), bf16),
+            pltpu.VMEM((2, own, CORES, group, rank, points2), bf16),
+            pltpu.VMEM((2, own, tiles, rank, points2), bf16),
             pltpu.VMEM((2, own, CORES, half_rows, points2), bf16),
             dma((4, own)), dma((4, own)), dma((4, own)),
-            dma((2, own, steps)), dma((2, own, steps)),
+            dma((2, own, group)), dma((2, own, group)), dma((2, own, tiles)),
+            dma((2, own)), dma((2, own, CORES)), dma((2, own, CORES, group)),
             dma((2, own)), dma((2, own)),
         ],
         compiler_params=pltpu.CompilerParams(

time: 30 us -> 28.6 us (0.953)
  Pallas kernels: 29.1 us -> 27.7 us
    pallas_call x1, Pallas kernels: 28.3 us -> 26.9 us  [body(): pl.pallas_call(kernel, out_shape=(pltpu.VMEM(out.shape, bf16), pltpu.VMEM...]
where the time goes in v3:
time: 28.6 us; the launch traced here: 28.4 us
  Pallas kernels  27.7 us (97%)
  between operations  0.64 us (2%)
    pallas_call x1, Pallas kernels, body(): pl.pallas_call(kernel, out_shape=(pltpu.VMEM(out.shape, bf16), pltpu.VMEM...  26.9 us
    pallas_call x1, Pallas kernels, body(): pl.pallas_call(copy_out, out_shape=(out, out), in_specs=[pl.BlockSpec(mem...  0.85 us

profile of v3, /device:TPU:0, one launch (start us, length us, event | category | flops | bytes accessed | tf_op | source)
XLA Modules:
  0.0 28.4 jit_solution(18293867082788500212)
XLA Ops:
  0.6 26.9 %shard_map.68 = (bf16[4,128,256]{2,1,0:T(8,128)(2,1)S(1)}, bf16[4,128,256]{2,1,0:T(8,128)(2,1)S(1)}) custom-call(s32[4,8,8]{2,1,0:T(8,128)} %class_ref.1, bf16[4,128,256]{2,1,0:T(8,128)(2,1)} %x_ref.1, bf16[4,128,256]{2,1,0:T(8,128)(2,1)} %r_ref.1, bf16[4,2,128,384]{3,2,1,0:T(8,128)(2,1)} %v_ref.1, bf16[4,2,128,384]{3,2,1,0:T(8,128)(2,1)} %u_ref.1), custom_call_target="tpu_custom_call" | custom-call | flops 805306368 | bytes 2621440 | tf_op jit(solution)/shard_map/pallas_call | solution.py:265
  27.5 0.9 %shard_map.69 = (bf16[4,128,256]{2,1,0:T(8,128)(2,1)}, bf16[4,128,256]{2,1,0:T(8,128)(2,1)}) custom-call(bf16[4,128,256]{2,1,0:T(8,128)(2,1)S(1)} %get-tuple-element.4.refs_0_, bf16[4,128,256]{2,1,0:T(8,128)(2,1)S(1)} %get-tuple-element.5.refs_1_), custom_call_target="tpu_custom_call" | custom-call | tf_op jit(solution)/shard_map/pallas_call | solution.py:291

commit v4 on v3

--- a/solution.py
+++ b/solution.py
@@ -61,15 +61,14 @@
 
     pairs = [(d, f) for d in range(2) for f in range(own)]
     through = pairs[:THROUGH]
-    for d, f in pairs:
-        local_load(2 * d, f).start()
-        local_load(2 * d + 1, f).start()
-
     barrier = pltpu.get_barrier_semaphore()
     pl.semaphore_signal(barrier, inc=1, device_id={"col": sibling}, device_id_type=MESH)
     for step in range(1, tiles):
         peer = ((tile + step) % tiles) * CORES + side
         pl.semaphore_signal(barrier, inc=1, device_id={"col": peer}, device_id_type=MESH)
+    for d, f in pairs:
+        local_load(2 * d, f).start()
+        local_load(2 * d + 1, f).start()
     pl.semaphore_wait(barrier, tiles)
 
     for d, f in pairs:

time: 28.6 us -> 28.6 us (level)
  no operation moved by 1% of the time
where the time goes in v4:
time: 28.6 us; the launch traced here: 28.4 us
  Pallas kernels  27.7 us (97%)
  between operations  0.64 us (2%)
    pallas_call x1, Pallas kernels, body(): pl.pallas_call(kernel, out_shape=(pltpu.VMEM(out.shape, bf16), pltpu.VMEM...  26.9 us
    pallas_call x1, Pallas kernels, body(): pl.pallas_call(copy_out, out_shape=(out, out), in_specs=[pl.BlockSpec(mem...  0.85 us

profile of v4, /device:TPU:0, one launch (start us, length us, event | category | flops | bytes accessed | tf_op | source)
XLA Modules:
  0.0 28.4 jit_solution(6818776657171605364)
XLA Ops:
  0.6 26.9 %shard_map.68 = (bf16[4,128,256]{2,1,0:T(8,128)(2,1)S(1)}, bf16[4,128,256]{2,1,0:T(8,128)(2,1)S(1)}) custom-call(s32[4,8,8]{2,1,0:T(8,128)} %class_ref.1, bf16[4,128,256]{2,1,0:T(8,128)(2,1)} %x_ref.1, bf16[4,128,256]{2,1,0:T(8,128)(2,1)} %r_ref.1, bf16[4,2,128,384]{3,2,1,0:T(8,128)(2,1)} %v_ref.1, bf16[4,2,128,384]{3,2,1,0:T(8,128)(2,1)} %u_ref.1), custom_call_target="tpu_custom_call" | custom-call | flops 805306368 | bytes 2621440 | tf_op jit(solution)/shard_map/pallas_call | solution.py:264
  27.5 0.9 %shard_map.69 = (bf16[4,128,256]{2,1,0:T(8,128)(2,1)}, bf16[4,128,256]{2,1,0:T(8,128)(2,1)}) custom-call(bf16[4,128,256]{2,1,0:T(8,128)(2,1)S(1)} %get-tuple-element.4.refs_0_, bf16[4,128,256]{2,1,0:T(8,128)(2,1)S(1)} %get-tuple-element.5.refs_1_), custom_call_target="tpu_custom_call" | custom-call | tf_op jit(solution)/shard_map/pallas_call | solution.py:290
